TPU v7x, 128 devices: a whole 4x4x4 slice. The times are simulated.
128 devices in a mesh: gx: 16 (over y, x), gy: 4 (over z), gz: 2 (over core).
Axes of the slice: x: 4, y: 4, z: 4, core: 2. Of those that a mesh axis runs over, the one named last changes fastest.
Arguments:
- velocity: float32 [3, 32, 256, 8192], P(None, 'gz', 'gx', 'gy'), may hold values from -6 to 6
- blade_pos: float32 [256, 3, 128], P(('gx', 'gy', 'gz')), as said below
- block_turbine: int32 [256], P(('gx', 'gy', 'gz')), may hold values from 0 to 3, as said below
- blade_vel: float32 [256, 3, 128], P(('gx', 'gy', 'gz')), may hold values from -6 to 6
- lift_coeff: float32 [256, 128], P(('gx', 'gy', 'gz')), may hold values from 0.2 to 2
Outputs:
- new_velocity: float32 [3, 32, 256, 8192], P(None, 'gz', 'gx', 'gy')
- point_force: float32 [256, 3, 128], P(('gx', 'gy', 'gz'))
Inputs may be any that keep to these rules, and one draw needn't show every extreme that they name: `block_turbine`: in each turbine row (blocks r * 4 * 2 * 2 onward, one row for each index of gx) every turbine number is named by exactly 4 blocks. `blade_pos`: the points of a block lie in its column: streamwise within its row's cells, spanwise within its turbine's cells, vertically between level 0 and the top level.
All inputs are finite; a program needn't handle non-finite values.
Results may differ from a plain program's by a relative error of at most 0.0003.
Values sent between devices are 32-bit elements; how exact they have to be, the bound alone decides.
A program may use at most 192 MiB of HBM per device.

v0:
```python
import math

import jax
import jax.numpy as jnp
from jax import lax
from jax.sharding import PartitionSpec as P

mean_wind = 1.0
viscosity = 0.2
smag_coeff = 0.17
time_step = 0.2
smear = 2.0
smear_norm = 1.0 / (smear**3 * math.pi**1.5)


def extended(cells, sides, width):
    for axis, dim in sides:
        count = lax.axis_size(axis)
        ends = count - 1
        head = lax.slice_in_dim(cells, 0, width, axis=dim)
        tail = lax.slice_in_dim(cells, cells.shape[dim] - width, cells.shape[dim], axis=dim)
        cells = jnp.concatenate(
            [
                lax.ppermute(tail, axis, [(i, (i + 1) % count) for i in range(ends)]),
                cells,
                lax.ppermute(head, axis, [((i + 1) % count, i) for i in range(ends)]),
            ],
            axis=dim,
        )
    return cells


def shifted(padded, axis_dim, offset):
    slicer = [slice(None), slice(2, -2), slice(2, -2), slice(2, -2)]
    extent = padded.shape[axis_dim] - 4
    slicer[axis_dim] = slice(2 + offset, 2 + offset + extent)
    return padded[tuple(slicer)]


def derivative(padded, axis_dim):
    near = shifted(padded, axis_dim, 1) - shifted(padded, axis_dim, -1)
    far = shifted(padded, axis_dim, 2) - shifted(padded, axis_dim, -2)
    return (8.0 * near - far) / 12.0


def second(padded, axis_dim):
    return (
        -shifted(padded, axis_dim, 2)
        + 16.0 * shifted(padded, axis_dim, 1)
        - 30.0 * shifted(padded, axis_dim, 0)
        + 16.0 * shifted(padded, axis_dim, -1)
        - shifted(padded, axis_dim, -2)
    ) / 12.0


def tendency(padded, body_force):
    along_x = derivative(padded, 2)
    along_y = derivative(padded, 3)
    along_z = derivative(padded, 1)
    gradients = (along_x, along_y, along_z)
    strain_sq = jnp.zeros(along_x.shape[1:], jnp.float32)
    for row_comp in range(3):
        for col_comp in range(3):
            strain = 0.5 * (gradients[col_comp][row_comp] + gradients[row_comp][col_comp])
            strain_sq = strain_sq + strain * strain
    eddy_visc = smag_coeff * smag_coeff * jnp.sqrt(2.0 * strain_sq)
    laplacian = second(padded, 1) + second(padded, 2) + second(padded, 3)
    return -mean_wind * along_x + (viscosity + eddy_visc[None]) * laplacian + body_force


def blade_force(sampled, blade_vel, lift_coeff):
    relative = sampled - blade_vel
    rel_speed = jnp.sqrt(jnp.sum(relative * relative, axis=1, keepdims=True))
    return -lift_coeff[:, None, :] * rel_speed * relative


def profile(anchor, count, centers):
    cells = (anchor + jnp.arange(count, dtype=jnp.int32)).astype(jnp.float32)
    gap = cells[:, None] - centers[None, :]
    return jnp.exp(-gap * gap / (smear * smear))


def local(velocity, blade_pos, block_turbine, blade_vel, lift_coeff):
    high = lax.Precision.HIGHEST
    components, depth_cells, row_cells, col_cells = velocity.shape
    owned_count = blade_pos.shape[0]
    point_count = blade_pos.shape[2]
    group_size = lax.axis_size(("gy", "gz"))
    row_blocks = owned_count * group_size
    per_turbine = row_blocks // lax.axis_size("gy")
    count = per_turbine * point_count
    turbine = lax.axis_index("gy")
    level_start = lax.axis_index("gz") * depth_cells
    row_start = lax.axis_index("gx") * row_cells
    col_start = turbine * col_cells
    padded = extended(velocity, (("gz", 1), ("gx", 2), ("gy", 3)), 2)
    row_pos, row_turb = (
        lax.all_gather(blade_pos, ("gy", "gz"), axis=0, tiled=True),
        lax.all_gather(block_turbine, ("gy", "gz"), axis=0, tiled=True),
    )
    matched = (row_turb == turbine).astype(jnp.int32)
    ranks = jnp.cumsum(matched) - 1
    slot_range = jnp.arange(per_turbine, dtype=jnp.int32)
    picker = ((ranks[None, :] == slot_range[:, None]) & (matched[None, :] == 1)).astype(jnp.float32)
    mine = jnp.einsum("ks,scp->kcp", picker, row_pos, precision=high)
    centers = mine.transpose(1, 0, 2).reshape(3, count)
    weight_x = profile(row_start, row_cells, centers[0])
    weight_y = profile(col_start, col_cells, centers[1])
    weight_z = profile(level_start, depth_cells, centers[2])
    plane = (weight_z[:, None, :] * weight_x[None, :, :]).reshape(depth_cells * row_cells, count)
    flat_vel = velocity.reshape(components * depth_cells * row_cells, col_cells)
    along = jnp.dot(flat_vel, weight_y, precision=high, preferred_element_type=jnp.float32)
    along = along.reshape(components, depth_cells * row_cells, count)
    partial_value = smear_norm * jnp.sum(along * plane[None], axis=1)
    partial_value = partial_value.reshape(components, per_turbine, point_count).transpose(1, 0, 2)
    table = jnp.einsum("ks,kcp->scp", picker, partial_value, precision=high)
    sampled = lax.psum_scatter(table, ("gy", "gz"), scatter_dimension=0, tiled=True)
    forces = blade_force(sampled, blade_vel, lift_coeff)
    row_force = lax.all_gather(forces, ("gy", "gz"), axis=0, tiled=True)
    slot_force = jnp.einsum("ks,scp->kcp", picker, row_force, precision=high)
    flat_force = slot_force.transpose(1, 0, 2).reshape(components, count)
    weighted = (smear_norm * flat_force[:, None, :] * plane[None]).reshape(
        components * depth_cells * row_cells, count
    )
    body_force = lax.dot_general(
        weighted,
        weight_y,
        (((1,), (1,)), ((), ())),
        precision=high,
        preferred_element_type=jnp.float32,
    )
    body_force = body_force.reshape(components, depth_cells, row_cells, col_cells)
    new_velocity = velocity + time_step * tendency(padded, body_force)
    return (new_velocity, forces)


def solution(mesh):
    in_specs = (
        P(None, "gz", "gx", "gy"),
        P(("gx", "gy", "gz"), None, None),
        P(("gx", "gy", "gz")),
        P(("gx", "gy", "gz"), None, None),
        P(("gx", "gy", "gz"), None),
    )
    out_specs = (P(None, "gz", "gx", "gy"), P(("gx", "gy", "gz"), None, None))
    return jax.shard_map(local, mesh=mesh, in_specs=in_specs, out_specs=out_specs, check_vma=False)
```

profile of v0, /device:TPU:25, one launch (start us, length us, event | category | flops | bytes accessed | tf_op | source)
XLA Modules:
  0.0 269.9 jit_solution(12857764865744317713)
XLA Ops:
  0.6 2.7 fusion.72
  4.6 4.8 %collective-permute-start.1 = (f32[3,2,16,2048]{3,2,1,0:T(8,128)}, f32[3,2,16,2048]{3,2,1,0:T(8,128)}, u32[]{:S(2)}, u32[]{:S(2)}) collective-permute-start(f32[3,2,16,2048]{3,2,1,0:T(8,128)} %get-tuple-element.11), channel_id=1, source_target_pairs={{1,0},{3,2},{5,4},{7,6},{9,8},{11,10},{13,12},{15,14},{17,16},{19,... | collective-permute-start | bytes 2359304 | tf_op jit(solution)/shard_map/ppermute | solution.py:26
  12.2 8.8 %all-reduce = s32[16]{0:T(128)S(1)} all-reduce(s32[16]{0:T(128)S(1)} %dynamic-update-slice), channel_id=1, replica_groups=mesh['gx'=16,'gy'=4,'gz'=2] {'gy','gz'}, use_global_device_ids=true, to_apply=%add | all-reduce | flops 16 | bytes 128
  22.0 14.4 %all_gather.10 = f32[16,3,128]{2,1,0:T(4,128)S(1)} all-gather(f32[2,3,128]{2,1,0:T(4,128)S(1)} %copy.16), channel_id=1, replica_groups=mesh['gx'=16,'gy'=4,'gz'=2] {'gy','gz'}, dimensions={0}, use_global_device_ids=true | all-gather | bytes 27648 | tf_op jit(solution)/shard_map/all_gather | solution.py:98
  36.5 24.0 %fusion.48 = f32[768,512]{0,1:T(8,128)S(1)} fusion(f32[768,2048]{1,0:T(8,128)} %bitcast.45, f32[512]{0:T(512)S(1)} %get-tuple-element.19, f32[2048]{0:T(1024)S(1)} %add_convert_fusion), kind=kOutput, calls=%fused_computation.67 | convolution fusion | flops 9667870720 | bytes 7874560 | tf_op jit(solution)/shard_map/dot_general | solution.py:112
  62.8 20.4 %all-reduce.1 = f32[16,3,128]{2,0,1:T(8,128)S(1)} all-reduce(f32[16,3,128]{2,0,1:T(8,128)S(1)} %fusion.60), channel_id=2, replica_groups=mesh['gx'=16,'gy'=4,'gz'=2] {'gy','gz'}, use_global_device_ids=true, to_apply=%region_2.3.clone | all-reduce | flops 6144 | bytes 49152
  83.3 16.3 %all_gather.11 = f32[16,3,128]{2,1,0:T(4,128)S(1)} all-gather(f32[2,3,128]{2,1,0:T(4,128)S(1)} %copy.19), channel_id=1, replica_groups=mesh['gx'=16,'gy'=4,'gz'=2] {'gy','gz'}, dimensions={0}, use_global_device_ids=true | all-gather | bytes 27648 | tf_op jit(solution)/shard_map/all_gather | solution.py:119
  99.6 2.5 constant_dynamic-update-slice_fusion.6
  102.1 11.8 %constant_dynamic-update-slice_fusion.4 = (f32[3,18,16,2048]{3,2,1,0:T(8,128)}, f32[3,18,16,2048]{3,2,1,0:T(8,128)}, f32[3,20,16,2048]{3,2,1,0:T(8,128)}) fusion(f32[3,16,16,2048]{3,2,1,0:T(8,128)} %param.5, f32[3,18,16,2048]{3,2,1,0:T(8,128)} %get-tuple-element.15, f32[3,20,16,2048]{3,2,1,0:T(8,128)} %get-tuple-element.16), kind=kLoop, calls=%fused_computation.89 | loop fusion | bytes 25165824
  114.0 2.5 constant_dynamic-update-slice_fusion.3
  116.5 4.5 %fusion.71 = (f32[3,20,2,2048]{3,2,1,0:T(2,128)S(1)}, f32[3,20,2,2048]{3,2,1,0:T(2,128)S(1)}) fusion(f32[3,20,16,2048]{3,2,1,0:T(8,128)} %get-tuple-element.14), kind=kLoop, calls=%fused_computation.115 | loop fusion | bytes 3932160 | tf_op jit(solution)/shard_map/slice | solution.py:21
  120.9 4.6 %collective-permute-start.2 = (f32[3,20,2,2048]{3,2,1,0:T(2,128)S(1)}, f32[3,20,2,2048]{3,2,1,0:T(2,128)S(1)}, u32[]{:S(2)}, u32[]{:S(2)}) collective-permute-start(f32[3,20,2,2048]{3,2,1,0:T(2,128)S(1)} %get-tuple-element.7), channel_id=1, source_target_pairs={{8,0},{16,8},{24,16},{32,24},{40,32},{48,40},{56,48},{64,56},{72,6... | collective-permute-start | bytes 2949128 | tf_op jit(solution)/shard_map/ppermute | solution.py:26
  125.5 1.9 collective-permute-start.3
  127.6 12.9 %subtract_multiply_fusion = f32[3,16,16,2048]{3,2,1,0:T(8,128)} fusion(f32[3,18,16,2048]{3,2,1,0:T(8,128)} %get-tuple-element.9, f32[3,18,16,2048]{3,2,1,0:T(8,128)} %get-tuple-element.13), kind=kLoop, calls=%fused_computation.18 | loop fusion | flops 7864320 | bytes 31457280 | tf_op jit(solution)/shard_map/div | solution.py:43
  140.5 6.0 %collective-permute-done.2 = f32[3,20,2,2048]{3,2,1,0:T(2,128)S(1)} collective-permute-done((f32[3,20,2,2048]{3,2,1,0:T(2,128)S(1)}, f32[3,20,2,2048]{3,2,1,0:T(2,128)S(1)}, u32[]{:S(2)}, u32[]{:S(2)}) %collective-permute-start.2) | collective-permute-done | bytes 983072 | tf_op jit(solution)/shard_map/ppermute | solution.py:26
  146.4 5.9 %collective-permute-done.3 = f32[3,20,2,2048]{3,2,1,0:T(2,128)S(1)} collective-permute-done((f32[3,20,2,2048]{3,2,1,0:T(2,128)S(1)}, f32[3,20,2,2048]{3,2,1,0:T(2,128)S(1)}, u32[]{:S(2)}, u32[]{:S(2)}) %collective-permute-start.3) | collective-permute-done | bytes 983072 | tf_op jit(solution)/shard_map/ppermute | solution.py:24
  153.7 1.6 copy.11
  157.0 4.2 %collective-permute-start.5 = (f32[3,20,20,2]{2,3,1,0:T(2,128)S(1)}, f32[3,20,20,2]{2,3,1,0:T(2,128)S(1)}, u32[]{:S(2)}, u32[]{:S(2)}) collective-permute-start(f32[3,20,20,2]{2,3,1,0:T(2,128)S(1)} %copy.13), channel_id=1, source_target_pairs={{0,2},{2,4},{4,6},{1,3},{3,5},{5,7},{8,10},{10,12},{12,14},{9,11},... | collective-permute-start | bytes 28808 | tf_op jit(solution)/shard_map/ppermute | solution.py:24
  161.3 15.6 %fusion.7 = f32[3,16,16,2048]{3,2,1,0:T(8,128)} fusion(f32[3,20,2,2048]{3,2,1,0:T(2,128)S(1)} %collective-permute-done.2, f32[3,20,16,2048]{3,2,1,0:T(8,128)} %get-tuple-element.14, f32[3,20,2,2048]{3,2,1,0:T(2,128)S(1)} %collective-permute-done.3), kind=kLoop, calls=%fused_computation.21 | loop fusion | flops 14155776 | bytes 16121856 | tf_op jit(solution)/shard_map/div | solution.py:43
  176.9 1.4 copy.12
  179.6 21.2 %pad_maximum_fusion = (f32[3,20,20,2050]{3,2,1,0:T(8,128)}, f32[3,20,20,2050]{3,2,1,0:T(8,128)}) fusion(f32[3,20,20,2]{3,2,1,0:T(8,128)} %copy.12, f32[3,20,2,2048]{3,2,1,0:T(2,128)S(1)} %collective-permute-done.2, f32[3,20,16,2048]{3,2,1,0:T(8,128)} %get-tuple-element.14, f32[3,20,2,2048]{3,2,1,0:T(2,128)} %copy-done, f32[3,20,20,2]{3,2,1,0:T(8,128)} %copy.14), kind=kLoop, calls=%fused_computation | loop fusion | flops 14760000 | bytes 29529600 | tf_op jit(solution)/shard_map/concatenate | solution.py:22
  200.8 18.2 %subtract_multiply_fusion.1 = f32[3,16,16,2048]{3,2,1,0:T(8,128)} fusion(f32[3,20,20,2050]{3,2,1,0:T(8,128)} %get-tuple-element.3, f32[3,20,20,2050]{3,2,1,0:T(8,128)} %get-tuple-element.2), kind=kLoop, calls=%fused_computation.19 | loop fusion | flops 7864320 | bytes 31457280 | tf_op jit(solution)/shard_map/div | solution.py:43
  219.0 6.9 %fusion.23 = f32[16,16,2048]{2,1,0:T(8,128)} fusion(f32[3,16,16,2048]{3,2,1,0:T(8,128)} %subtract_multiply_fusion, f32[3,16,16,2048]{3,2,1,0:T(8,128)} %subtract_multiply_fusion.1, f32[3,16,16,2048]{3,2,1,0:T(8,128)S(1)} %bitcast.44), kind=kLoop, calls=%fused_computation.36 | loop fusion | flops 15728640 | bytes 20971520 | tf_op jit(solution)/shard_map/mul | solution.py:68
  225.9 43.8 %fusion.4 = f32[3,16,16,2048]{3,2,1,0:T(8,128)} fusion(f32[3,16,16,2048]{3,2,1,0:T(8,128)} %param.5, f32[3,20,20,2050]{3,2,1,0:T(8,128)} %get-tuple-element.3, f32[3,20,20,2050]{3,2,1,0:T(8,128)} %get-tuple-element.2, f32[3,18,16,2048]{3,2,1,0:T(8,128)} %get-tuple-element.9, f32[3,18,16,2048]{3,2,1,0:T(8,128)} %get-tuple-element.13, ...), kind=kOutput, calls=%fused_computation.13 | convolution fusion | flops 9728032768 | bytes 75382784 | tf_op jit(solution)/shard_map/dot_general | solution.py:125
  (55 shorter events, 10.9 us)
Async XLA Ops:
  3.3 96.3 %collective-permute-start = (f32[3,2,16,2048]{3,2,1,0:T(8,128)}, f32[3,2,16,2048]{3,2,1,0:T(8,128)}, u32[]{:S(2)}, u32[]{:S(2)}) collective-permute-start(f32[3,2,16,2048]{3,2,1,0:T(8,128)} %get-tuple-element.12), channel_id=1, source_target_pairs={{0,1},{2,3},{4,5},{6,7},{8,9},{10,11},{12,13},{14,15},{16,17},{18,... | collective-permute-start | bytes 2359304 | tf_op jit(solution)/shard_map/ppermute | solution.py:24
  4.6 109.3 %collective-permute-start.1 = (f32[3,2,16,2048]{3,2,1,0:T(8,128)}, f32[3,2,16,2048]{3,2,1,0:T(8,128)}, u32[]{:S(2)}, u32[]{:S(2)}) collective-permute-start(f32[3,2,16,2048]{3,2,1,0:T(8,128)} %get-tuple-element.11), channel_id=1, source_target_pairs={{1,0},{3,2},{5,4},{7,6},{9,8},{11,10},{13,12},{15,14},{17,16},{19,... | collective-permute-start | bytes 2359304 | tf_op jit(solution)/shard_map/ppermute | solution.py:26
  36.5 46.7 %copy-start.3 = (f32[2,3,128]{2,0,1:T(2,128)S(1)}, f32[2,3,128]{2,0,1:T(2,128)}, u32[]{:S(2)}) copy-start(f32[2,3,128]{2,0,1:T(2,128)} %param.8) | copy-start | bytes 9220
  36.5 46.7 %copy-start.4 = (f32[2,128]{1,0:T(2,128)S(1)}, f32[2,128]{1,0:T(2,128)}, u32[]{:S(2)}) copy-start(f32[2,128]{1,0:T(2,128)} %param.9) | copy-start | bytes 3076
  61.1 0.8 copy-start.1
  83.3 30.7 %copy-start.2 = (f32[2,3,128]{2,0,1:T(2,128)}, f32[2,3,128]{2,0,1:T(2,128)S(1)}, u32[]{:S(2)}) copy-start(f32[2,3,128]{2,0,1:T(2,128)S(1)} %broadcast_multiply_fusion.2) | copy-start | bytes 9220
  116.4 35.9 %slice-start = ((s8[7864320]{0:T(1024)(128)(4,1)}), s8[4194304]{0:T(1024)(128)(4,1)S(1)}, s32[]{:S(2)}) async-start(s8[7864320]{0:T(1024)(128)(4,1)} %bitcast.41), calls=%async_computation | async-start | bytes 8388608
  120.9 25.5 %collective-permute-start.2 = (f32[3,20,2,2048]{3,2,1,0:T(2,128)S(1)}, f32[3,20,2,2048]{3,2,1,0:T(2,128)S(1)}, u32[]{:S(2)}, u32[]{:S(2)}) collective-permute-start(f32[3,20,2,2048]{3,2,1,0:T(2,128)S(1)} %get-tuple-element.7), channel_id=1, source_target_pairs={{8,0},{16,8},{24,16},{32,24},{40,32},{48,40},{56,48},{64,56},{72,6... | collective-permute-start | bytes 2949128 | tf_op jit(solution)/shard_map/ppermute | solution.py:26
  125.5 26.8 %collective-permute-start.3 = (f32[3,20,2,2048]{3,2,1,0:T(2,128)S(1)}, f32[3,20,2,2048]{3,2,1,0:T(2,128)S(1)}, u32[]{:S(2)}, u32[]{:S(2)}) collective-permute-start(f32[3,20,2,2048]{3,2,1,0:T(2,128)S(1)} %get-tuple-element.6), channel_id=1, source_target_pairs={{0,8},{8,16},{16,24},{24,32},{32,40},{40,48},{48,56},{56,64},{64,7... | collective-permute-start | bytes 2949128 | tf_op jit(solution)/shard_map/ppermute | solution.py:24
  127.6 24.8 %slice-start.1 = ((s8[7864320]{0:T(1024)(128)(4,1)}), s8[3670016]{0:T(1024)(128)(4,1)S(1)}, s32[]{:S(2)}) async-start(s8[7864320]{0:T(1024)(128)(4,1)} %bitcast.41), calls=%async_computation.1 | async-start | bytes 7340032
  152.3 8.9 %copy-start = (f32[3,20,2,2048]{3,2,1,0:T(2,128)}, f32[3,20,2,2048]{3,2,1,0:T(2,128)S(1)}, u32[]{:S(2)}) copy-start(f32[3,20,2,2048]{3,2,1,0:T(2,128)S(1)} %collective-permute-done.3) | copy-start | bytes 2949124
  155.3 21.6 %collective-permute-start.4 = (f32[3,20,20,2]{2,3,1,0:T(2,128)S(1)}, f32[3,20,20,2]{2,3,1,0:T(2,128)S(1)}, u32[]{:S(2)}, u32[]{:S(2)}) collective-permute-start(f32[3,20,20,2]{2,3,1,0:T(2,128)S(1)} %copy.11), channel_id=1, source_target_pairs={{2,0},{4,2},{6,4},{3,1},{5,3},{7,5},{10,8},{12,10},{14,12},{11,9},... | collective-permute-start | bytes 28808 | tf_op jit(solution)/shard_map/ppermute | solution.py:26
  157.0 21.2 %collective-permute-start.5 = (f32[3,20,20,2]{2,3,1,0:T(2,128)S(1)}, f32[3,20,20,2]{2,3,1,0:T(2,128)S(1)}, u32[]{:S(2)}, u32[]{:S(2)}) collective-permute-start(f32[3,20,20,2]{2,3,1,0:T(2,128)S(1)} %copy.13), channel_id=1, source_target_pairs={{0,2},{2,4},{4,6},{1,3},{3,5},{5,7},{8,10},{10,12},{12,14},{9,11},... | collective-permute-start | bytes 28808 | tf_op jit(solution)/shard_map/ppermute | solution.py:24
  178.3 40.7 %slice-start.2 = ((s8[6291456]{0:T(1024)(128)(4,1)}), s8[2097152]{0:T(1024)(128)(4,1)S(1)}, s32[]{:S(2)}) async-start(s8[6291456]{0:T(1024)(128)(4,1)} %bitcast.43), calls=%async_computation.2 | async-start | bytes 4194304
  179.6 39.4 %slice-start.3 = ((s8[6291456]{0:T(1024)(128)(4,1)}), s8[4194304]{0:T(1024)(128)(4,1)S(1)}, s32[]{:S(2)}) async-start(s8[6291456]{0:T(1024)(128)(4,1)} %bitcast.43), calls=%async_computation.3 | async-start | bytes 8388608
where the time goes:
time: 272 us; the launch traced here: 270 us
  other arithmetic  76.7 us (28%)
  matrix products  68.2 us (25%)
  blocking collectives  59.9 us (22%)
  local copies, waits for them, and re-layouts  32.8 us (12%)
  starting transfers between devices  18.1 us (7%)
  waiting for transfers between devices  11.9 us (4%)
    div x3, other arithmetic, derivative(): return (8.0 * near - far) / 12.0  46.7 us
    dot_general x1, matrix products, local(): lax.dot_general(weighted, weight_y, (((1,), (1,)), ((), ())), precision=h...  43.8 us
    unnamed x2, blocking collectives  29.2 us
    dot_general x1, matrix products, local(): jnp.dot(flat_vel, weight_y, precision=high, preferred_element_type=jnp.fl...  24 us
    concatenate x1, other arithmetic, extended(): jnp.concatenate([lax.ppermute(tail, axis, [(i, (i + 1) % count) for i in...  21.2 us
    unnamed x25, local copies, waits for them, and re-layouts  17.8 us
    all_gather x1, blocking collectives, local(): row_force = lax.all_gather(forces, ('gy', 'gz'), axis=0, tiled=True)  16.3 us
    all_gather x1, blocking collectives, local(): lax.all_gather(blade_pos, ('gy', 'gz'), axis=0, tiled=True)  14.4 us
  transfers between devices with their start and end apart: 6, of which 2 were waited for; matrix products, arithmetic and copies ran while one was open for 27% of the time, Pallas kernels for 0%

commit v1 on v0

v1 whole, which is shorter than its diff:
```python
import functools
import math

import jax
import jax.numpy as jnp
from jax import lax
from jax.experimental import pallas as pl
from jax.experimental.pallas import tpu as pltpu
from jax.sharding import PartitionSpec as P

mean_wind = 1.0
viscosity = 0.2
smag_coeff = 0.17
time_step = 0.2
smear = 2.0
smear_norm = 1.0 / (smear**3 * math.pi**1.5)

F32, BF16 = jnp.float32, jnp.bfloat16
MESH = pl.DeviceIdType.MESH
LANES = 128
TOP = 8


def split(value):
    high = value.astype(BF16)
    return high, (value - high.astype(F32)).astype(BF16)


def gaussian(start, count, centers):
    cells = (lax.broadcasted_iota(jnp.int32, (count, 1), 0) + start).astype(F32)
    gap = cells - centers
    return jnp.exp(gap * gap * (-1.0 / (smear * smear)))


def stencil(win, tile, z, body):
    lane = lax.broadcasted_iota(jnp.int32, (16, LANES), 1)
    grads, laps, own = [], [], []
    for c in range(3):
        def rows(offset, level=0, side=0, c=c):
            return win[tile + side, c, z + level, TOP + offset : TOP + offset + 16, :]

        u = rows(0)
        left, right = rows(0, side=-1), rows(0, side=1)
        y_p1 = pltpu.roll(jnp.where(lane < 1, right, u), LANES - 1, 1)
        y_p2 = pltpu.roll(jnp.where(lane < 2, right, u), LANES - 2, 1)
        y_m1 = pltpu.roll(jnp.where(lane >= LANES - 1, left, u), 1, 1)
        y_m2 = pltpu.roll(jnp.where(lane >= LANES - 2, left, u), 2, 1)
        pairs = (
            (rows(1), rows(-1), rows(2), rows(-2)),
            (y_p1, y_m1, y_p2, y_m2),
            (rows(0, 1), rows(0, -1), rows(0, 2), rows(0, -2)),
        )
        grads.append([8.0 * (p1 - m1) - (p2 - m2) for p1, m1, p2, m2 in pairs])
        near = sum(p1 + m1 for p1, m1, _, _ in pairs[1:]) + (pairs[0][0] + pairs[0][1])
        far = sum(p2 + m2 for _, _, p2, m2 in pairs[1:]) + (pairs[0][2] + pairs[0][3])
        laps.append(16.0 * near - far - 90.0 * u)
        own.append(u)
    diag = sum(grads[i][i] * grads[i][i] for i in range(3))
    cross = jnp.zeros((16, LANES), F32)
    for i, j in ((0, 1), (0, 2), (1, 2)):
        both = grads[i][j] + grads[j][i]
        cross = cross + both * both
    strain = diag + diag + cross
    nu = viscosity * time_step / 12.0 + (smag_coeff * smag_coeff * time_step / 144.0) * jnp.sqrt(strain)
    outs = []
    for c in range(3):
        outs.append(own[c] + (-mean_wind * time_step / 12.0) * grads[c][0] + nu * laps[c] + time_step * body[c])
    return outs


def kernel(
    sizes, v, pos, turb, bvel, lift, out, pf,
    win, table, whi, wlo, along, plane, ghi, glo, part, other, back, owned,
    load_sem, tab_send, tab_recv, z_send, z_recv, x_send, x_recv, y_send, y_recv,
    part_sem, back_send, back_recv,
):
    n_gx, n_gy, n_gz = sizes
    gx, gy, gz = lax.axis_index("gx"), lax.axis_index("gy"), lax.axis_index("gz")
    mine = gy * n_gz + gz
    group = n_gy * n_gz
    _, depth, nrow, ncol = v.shape
    tiles = ncol // LANES
    own_blocks = pos.shape[0]
    blocks = group * own_blocks
    per_turbine = blocks // n_gy
    pts = pos.shape[2]
    count = per_turbine * pts
    rows = 3 * depth * nrow

    barrier = pltpu.get_barrier_semaphore()
    for step in range(1, group):
        peer = lax.rem(mine + step, group)
        pl.semaphore_signal(
            barrier, 1, device_id={"gy": peer // n_gz, "gz": lax.rem(peer, n_gz)}, device_id_type=MESH
        )

    @pl.when(gx > 0)
    def _():
        pl.semaphore_signal(barrier, 1, device_id={"gx": gx - 1}, device_id_type=MESH)

    @pl.when(gx < n_gx - 1)
    def _():
        pl.semaphore_signal(barrier, 1, device_id={"gx": gx + 1}, device_id_type=MESH)

    def lanes(t):
        return pl.ds(pl.multiple_of(t * LANES, LANES), LANES)

    def load(t):
        return pltpu.make_async_copy(
            v.at[:, :, :, lanes(t)], win.at[t + 1, :, pl.ds(2, depth), pl.ds(TOP, nrow), :], load_sem.at[t]
        )

    @pl.loop(0, tiles)
    def _(t):
        load(t).start()

    for b in range(own_blocks):
        at = mine * own_blocks + b
        table[at, 0:3, :] = pos[b]
        table[at, 3:6, :] = bvel[b]
        table[at, 6:7, :] = lift[b : b + 1, :]
        table[at, 7:8, :] = jnp.full((1, pts), turb[b].astype(F32))

    z_gap = jnp.where(gz == 0, 0, depth + 2)

    @pl.loop(0, tiles)
    def _(t):
        for c in range(3):
            for k in range(2):
                win[t + 1, c, z_gap + k, TOP : TOP + nrow, :] = jnp.zeros((nrow, LANES), F32)

    @pl.when(gx == 0)
    def _():
        @pl.loop(0, tiles)
        def _(t):
            win[t + 1, :, 2 : 2 + depth, TOP - 2 : TOP, :] = jnp.zeros((3, depth, 2, LANES), F32)

    @pl.when(gx == n_gx - 1)
    def _():
        @pl.loop(0, tiles)
        def _(t):
            win[t + 1, :, 2 : 2 + depth, TOP + nrow : TOP + nrow + 2, :] = jnp.zeros((3, depth, 2, LANES), F32)

    @pl.when(gy == 0)
    def _():
        win[0, :, 2 : 2 + depth, TOP : TOP + nrow, :] = jnp.zeros((3, depth, nrow, LANES), F32)

    @pl.when(gy == n_gy - 1)
    def _():
        win[tiles + 1, :, 2 : 2 + depth, TOP : TOP + nrow, :] = jnp.zeros((3, depth, nrow, LANES), F32)

    pl.semaphore_wait(barrier, group - 1 + (gx > 0).astype(jnp.int32) + (gx < n_gx - 1).astype(jnp.int32))

    def remote(src, dst, send, recv, device):
        return pltpu.make_async_remote_copy(
            src_ref=src, dst_ref=dst, send_sem=send, recv_sem=recv, device_id=device, device_id_type=MESH
        )

    own_slots = pl.ds(mine * own_blocks, own_blocks)

    def tab(step):
        peer = lax.rem(mine + step, group)
        return remote(
            table.at[own_slots], table.at[own_slots], tab_send.at[step], tab_recv.at[step],
            {"gy": peer // n_gz, "gz": lax.rem(peer, n_gz)},
        )

    z_from = jnp.where(gz == 0, depth - 2, 0)
    z_to = jnp.where(gz == 0, 0, depth + 2)

    def z_copy(t):
        return remote(
            v.at[:, pl.ds(z_from, 2), :, lanes(t)],
            win.at[t + 1, :, pl.ds(z_to, 2), pl.ds(TOP, nrow), :],
            z_send.at[t], z_recv.at[t], {"gz": 1 - gz},
        )

    def x_up(t):
        return remote(
            v.at[:, :, pl.ds(nrow - 2, 2), lanes(t)],
            win.at[t + 1, :, pl.ds(2, depth), pl.ds(TOP - 2, 2), :],
            x_send.at[0, t], x_recv.at[0, t], {"gx": gx + 1},
        )

    def x_down(t):
        return remote(
            v.at[:, :, pl.ds(0, 2), lanes(t)],
            win.at[t + 1, :, pl.ds(2, depth), pl.ds(TOP + nrow, 2), :],
            x_send.at[1, t], x_recv.at[1, t], {"gx": gx - 1},
        )

    def y_copy(side):
        first = 0 if side else ncol - LANES
        return remote(
            v.at[:, :, :, pl.ds(first, LANES)],
            win.at[tiles + 1 if side else 0, :, pl.ds(2, depth), pl.ds(TOP, nrow), :],
            y_send.at[side], y_recv.at[side], {"gy": gy - 1 if side else gy + 1},
        )

    for step in range(1, group):
        tab(step).start()

    @pl.when(gy > 0)
    def _():
        y_copy(1).start()

    @pl.when(gy < n_gy - 1)
    def _():
        y_copy(0).start()

    @pl.loop(0, tiles)
    def _(t):
        @pl.when(gx < n_gx - 1)
        def _():
            x_up(t).start()

        @pl.when(gx > 0)
        def _():
            x_down(t).start()

        z_copy(t).start()

    for step in range(1, group):
        tab(step).wait_recv()
    turbine = gy.astype(F32)

    def matches():
        rank = jnp.zeros((8, pts), F32)
        for s in range(blocks):
            entry = table[s]
            match = jnp.broadcast_to(entry[7:8, :], (8, pts)) == turbine
            yield s, entry, [match & (rank == float(k)) for k in range(per_turbine)]
            rank = rank + jnp.where(match, 1.0, 0.0)

    slots = [jnp.zeros((8, pts), F32) for _ in range(per_turbine)]
    for _, entry, chosen in matches():
        slots = [jnp.where(one, entry, held) for one, held in zip(chosen, slots)]

    def flat(row):
        return jnp.concatenate([slot[row : row + 1, :] for slot in slots], axis=1)

    weight_x = gaussian(gx * nrow, nrow, flat(0))
    weight_z = gaussian(gz * depth, depth, flat(2))
    for z in range(depth):
        plane[z * nrow : (z + 1) * nrow, :] = weight_z[z : z + 1, :] * weight_x
    center_y = flat(1)

    step_cols = 2 * LANES
    steps = ncol // step_cols

    @pl.loop(0, steps)
    def _(j):
        at = pl.multiple_of(j * step_cols, step_cols)
        high, low = split(gaussian(gy * ncol + at, step_cols, center_y))
        whi[pl.ds(at, step_cols), :] = high
        wlo[pl.ds(at, step_cols), :] = low
        load(2 * j).wait()
        load(2 * j + 1).wait()
        cells = jnp.concatenate(
            [
                win[2 * j + 1 + k, :, 2 : 2 + depth, TOP : TOP + nrow, :].reshape(rows, LANES)
                for k in range(2)
            ],
            axis=1,
        )
        vhi, vlo = split(cells)
        dot = functools.partial(jnp.dot, preferred_element_type=F32)
        now = dot(vhi, high) + (dot(vhi, low) + dot(vlo, high))

        @pl.when(j == 0)
        def _():
            along[...] = now

        @pl.when(j > 0)
        def _():
            along[...] += now

    per_comp = depth * nrow
    part[3:8, :] = jnp.zeros((5, count), F32)
    for c in range(3):
        part[c : c + 1, :] = jnp.sum(
            along[c * per_comp : (c + 1) * per_comp, :] * plane[...], axis=0, keepdims=True
        )
    swap = remote(part, other, part_sem.at[0], part_sem.at[1], {"gz": 1 - gz})
    swap.start()
    swap.wait_recv()
    relative = [
        smear_norm * (part[c : c + 1, :] + other[c : c + 1, :]) - flat(3 + c) for c in range(3)
    ]
    speed = jnp.sqrt(relative[0] * relative[0] + relative[1] * relative[1] + relative[2] * relative[2])
    force = [-flat(6) * speed * relative[c] for c in range(3)]

    stacked = [
        jnp.concatenate(
            [force[c][:, k * pts : (k + 1) * pts] for c in range(3)] + [jnp.zeros((5, pts), F32)], axis=0
        )
        for k in range(per_turbine)
    ]
    for s, _, chosen in matches():
        back[s] = sum(jnp.where(one, held, 0.0) for one, held in zip(chosen, stacked))

    def give(step):
        peer = lax.rem(gy + step, n_gy)
        return remote(
            back.at[pl.ds((peer * n_gz + gz) * own_blocks, own_blocks)], owned.at[step],
            back_send.at[step], back_recv.at[step], {"gy": peer},
        )

    for step in range(1, n_gy):
        give(step).start()

    for c in range(3):
        high, low = split((smear_norm * force[c]) * plane[...])
        ghi[c * per_comp : (c + 1) * per_comp, :] = high
        glo[c * per_comp : (c + 1) * per_comp, :] = low

    @pl.when(gy > 0)
    def _():
        y_copy(0).wait_recv()

    @pl.when(gy < n_gy - 1)
    def _():
        y_copy(1).wait_recv()

    @pl.loop(0, steps)
    def _(j):
        at = pl.multiple_of(j * step_cols, step_cols)
        high, low = whi[pl.ds(at, step_cols), :], wlo[pl.ds(at, step_cols), :]

        def dot(a, b):
            return lax.dot_general(a, b, (((1,), (1,)), ((), ())), preferred_element_type=F32)

        along[:, 0:step_cols] = dot(ghi[...], high) + (dot(ghi[...], low) + dot(glo[...], high))
        for k in range(2):
            t = 2 * j + k

            @pl.when(gx > 0)
            def _():
                x_up(t).wait_recv()

            @pl.when(gx < n_gx - 1)
            def _():
                x_down(t).wait_recv()

            z_copy(t).wait_recv()

            @pl.loop(0, depth // 4)
            def _(zb):
                for dz in range(4):
                    z = zb * 4 + dz
                    body = [
                        along[
                            pl.ds(pl.multiple_of(c * per_comp + z * nrow, nrow), nrow),
                            k * LANES : (k + 1) * LANES,
                        ]
                        for c in range(3)
                    ]
                    new = stencil(win, t + 1, z + 2, body)
                    for c in range(3):
                        out[c, z, :, lanes(t)] = new[c]

    for step in range(1, n_gy):
        give(step).wait()
    total = back[own_slots] + sum(owned[step] for step in range(1, n_gy))
    pf[...] = total[:, 0:3, :]
    for step in range(1, group):
        tab(step).wait_send()
    swap.wait_send()

    @pl.when(gy > 0)
    def _():
        y_copy(1).wait_send()

    @pl.when(gy < n_gy - 1)
    def _():
        y_copy(0).wait_send()

    @pl.loop(0, tiles)
    def _(t):
        @pl.when(gx < n_gx - 1)
        def _():
            x_up(t).wait_send()

        @pl.when(gx > 0)
        def _():
            x_down(t).wait_send()

        z_copy(t).wait_send()


def local(sizes, velocity, blade_pos, block_turbine, blade_vel, lift_coeff):
    n_gx, n_gy, n_gz = sizes
    comps, depth, nrow, ncol = velocity.shape
    own_blocks, _, pts = blade_pos.shape
    tiles = ncol // LANES
    group = n_gy * n_gz
    blocks = group * own_blocks
    count = blocks // n_gy * pts
    rows = comps * depth * nrow
    dma = pltpu.SemaphoreType.DMA
    vmem = pl.BlockSpec(memory_space=pltpu.VMEM)
    return pl.pallas_call(
        functools.partial(kernel, sizes),
        out_shape=(
            jax.ShapeDtypeStruct(velocity.shape, F32),
            jax.ShapeDtypeStruct(blade_pos.shape, F32),
        ),
        in_specs=[
            pl.BlockSpec(memory_space=pl.ANY), vmem, pl.BlockSpec(memory_space=pltpu.SMEM), vmem, vmem,
        ],
        out_specs=(vmem, vmem),
        scratch_shapes=[
            pltpu.VMEM((tiles + 2, comps, depth + 4, nrow + 16, LANES), F32),
            pltpu.VMEM((blocks, 8, pts), F32),
            pltpu.VMEM((ncol, count), BF16),
            pltpu.VMEM((ncol, count), BF16),
            pltpu.VMEM((rows, count), F32),
            pltpu.VMEM((depth * nrow, count), F32),
            pltpu.VMEM((rows, count), BF16),
            pltpu.VMEM((rows, count), BF16),
            pltpu.VMEM((8, count), F32),
            pltpu.VMEM((8, count), F32),
            pltpu.VMEM((blocks, 8, pts), F32),
            pltpu.VMEM((n_gy, own_blocks, 8, pts), F32),
            dma((tiles,)),
            dma((group,)), dma((group,)),
            dma((tiles,)), dma((tiles,)),
            dma((2, tiles)), dma((2, tiles)),
            dma((2,)), dma((2,)),
            dma((2,)),
            dma((n_gy,)), dma((n_gy,)),
        ],
        compiler_params=pltpu.CompilerParams(
            collective_id=0, has_side_effects=True, vmem_limit_bytes=60 * 2**20
        ),
        name="evolve",
    )(velocity, blade_pos, block_turbine, blade_vel, lift_coeff)


def solution(mesh):
    sizes = tuple(mesh.shape[axis] for axis in ("gx", "gy", "gz"))
    in_specs = (
        P(None, "gz", "gx", "gy"),
        P(("gx", "gy", "gz"), None, None),
        P(("gx", "gy", "gz")),
        P(("gx", "gy", "gz"), None, None),
        P(("gx", "gy", "gz"), None),
    )
    out_specs = (P(None, "gz", "gx", "gy"), P(("gx", "gy", "gz"), None, None))
    return jax.shard_map(
        functools.partial(local, sizes), mesh=mesh, in_specs=in_specs, out_specs=out_specs, check_vma=False
    )
```

time: 272 us -> 55.9 us (0.21)
  other arithmetic: 76.7 us -> 0 us
  matrix products: 68.2 us -> 0 us
  blocking collectives: 59.9 us -> 0 us
  Pallas kernels: 0 us -> 44.9 us
  local copies, waits for them, and re-layouts: 32.8 us -> 10.1 us
  starting transfers between devices: 18.1 us -> 0 us
  waiting for transfers between devices: 11.9 us -> 0 us
    dot_general x5 -> x0, matrix products: 68.2 us -> none  [the longest x1 43.8 us: local(): lax.dot_general(weighted, weight_y, (((1,), (1,)), ((), ())), precision=h...]
    div x3 -> x0, other arithmetic: 46.7 us -> none  [derivative(): return (8.0 * near - far) / 12.0]
    pallas_call x0 -> x1, Pallas kernels: none -> 44.9 us  [local(): pl.pallas_call(functools.partial(kernel, sizes), out_shape=(jax.ShapeDtyp...]
    all_gather x2 -> x0, blocking collectives: 30.7 us -> none  [the longest x1 16.3 us: local(): row_force = lax.all_gather(forces, ('gy', 'gz'), axis=0, tiled=True)]
    unnamed x2 -> x0, blocking collectives: 29.2 us -> none
    concatenate x1 -> x0, other arithmetic: 21.2 us -> none  [extended(): jnp.concatenate([lax.ppermute(tail, axis, [(i, (i + 1) % count) for i in...]
    ppermute x6 -> x0, starting transfers between devices: 18.1 us -> none  [the longest x3 10.7 us: extended(): lax.ppermute(head, axis, [((i + 1) % count, i) for i in range(ends)])]
    ppermute x6 -> x0, waiting for transfers between devices: 11.9 us -> none  [the longest x3 5.97 us: extended(): lax.ppermute(head, axis, [((i + 1) % count, i) for i in range(ends)])]
  transfers between devices with their start and end apart: 6 -> 0, of which waited for: 2 -> 0; matrix products, arithmetic and copies ran while one was open for 27% -> 0% of each run, Pallas kernels for 0% -> 0%
where the time goes in v1:
time: 55.9 us; the launch traced here: 55.6 us
  Pallas kernels  44.9 us (80%)
  local copies, waits for them, and re-layouts  10.1 us (18%)
  between operations  0.64 us (1%)
    pallas_call x1, Pallas kernels, local(): pl.pallas_call(functools.partial(kernel, sizes), out_shape=(jax.ShapeDtyp...  44.9 us
    unnamed x3, local copies, waits for them, and re-layouts  8.83 us
    pallas_call x1, local copies, waits for them, and re-layouts, local(): pl.pallas_call(functools.partial(kernel, sizes), out_shape=(jax.ShapeDtyp...  1.26 us

profile of v1, /device:TPU:25, one launch (start us, length us, event | category | flops | bytes accessed | tf_op | source)
XLA Modules:
  0.0 55.6 jit_solution(9907174622121310120)
XLA Ops:
  0.6 1.3 %copy.7.pos = f32[2,3,128]{2,1,0:T(4,128)} copy(f32[2,3,128]{2,0,1:T(2,128)} %param.6) | data formatting | bytes 6144 | tf_op args[1]
  1.9 1.3 %copy.8.bvel = f32[2,3,128]{2,1,0:T(4,128)} copy(f32[2,3,128]{2,0,1:T(2,128)} %param.8) | data formatting | bytes 6144 | tf_op args[3]
  3.2 44.9 %evolve.1 = (f32[3,16,16,2048]{3,2,1,0:T(8,128)}, f32[2,3,128]{2,1,0:T(4,128)}) custom-call(f32[3,16,16,2048]{3,2,1,0:T(8,128)} %v.1, f32[2,3,128]{2,1,0:T(4,128)} %copy.7.pos, s32[2]{0:T(128)} %turb.1, f32[2,3,128]{2,1,0:T(4,128)} %copy.8.bvel, f32[2,128]{1,0:T(2,128)} %lift.1), custom_call_target="tpu_custom_call" | custom-call | tf_op jit(solution)/shard_map/evolve/pallas_call | solution.py:402
  48.1 1.3 %copy.9 = f32[2,3,128]{2,0,1:T(2,128)} copy(f32[2,3,128]{2,1,0:T(4,128)} %get-tuple-element.3) | data formatting | bytes 6144 | tf_op jit(solution)/shard_map/evolve/pallas_call | solution.py:402
  49.4 6.3 %copy.11 = f32[3,16,16,2048]{3,2,1,0:T(8,128)} copy(f32[3,16,16,2048]{3,2,1,0:T(8,128)} %get-tuple-element.6) | data formatting | bytes 12582912

commit v2 on v1

--- a/solution.py
+++ b/solution.py
@@ -69,9 +69,10 @@
 
 
 def kernel(
-    sizes, v, pos, turb, bvel, lift, out, pf,
+    sizes, v, pos_in, turb_in, bvel_in, lift_in, out, pf,
+    pos, turb, bvel, lift,
     win, table, whi, wlo, along, plane, ghi, glo, part, other, back, owned,
-    load_sem, tab_send, tab_recv, z_send, z_recv, x_send, x_recv, y_send, y_recv,
+    small_sem, load_sem, tab_send, tab_recv, z_send, z_recv, x_send, x_recv, y_send, y_recv,
     part_sem, back_send, back_recv,
 ):
     n_gx, n_gy, n_gz = sizes
@@ -80,13 +81,20 @@
     group = n_gy * n_gz
     _, depth, nrow, ncol = v.shape
     tiles = ncol // LANES
-    own_blocks = pos.shape[0]
+    own_blocks = pos.shape[1]
     blocks = group * own_blocks
     per_turbine = blocks // n_gy
     pts = pos.shape[2]
     count = per_turbine * pts
     rows = 3 * depth * nrow
 
+    small = [
+        pltpu.make_async_copy(src, dst, small_sem.at[i])
+        for i, (src, dst) in enumerate(((turb_in, turb), (pos_in, pos), (bvel_in, bvel), (lift_in, lift)))
+    ]
+    for copy in small:
+        copy.start()
+
     barrier = pltpu.get_barrier_semaphore()
     for step in range(1, group):
         peer = lax.rem(mine + step, group)
@@ -114,10 +122,13 @@
     def _(t):
         load(t).start()
 
+    for copy in small:
+        copy.wait()
     for b in range(own_blocks):
         at = mine * own_blocks + b
-        table[at, 0:3, :] = pos[b]
-        table[at, 3:6, :] = bvel[b]
+        for c in range(3):
+            table[at, c : c + 1, :] = pos[c, b : b + 1, :]
+            table[at, 3 + c : 4 + c, :] = bvel[c, b : b + 1, :]
         table[at, 6:7, :] = lift[b : b + 1, :]
         table[at, 7:8, :] = jnp.full((1, pts), turb[b].astype(F32))
 
@@ -362,7 +373,9 @@
     for step in range(1, n_gy):
         give(step).wait()
     total = back[own_slots] + sum(owned[step] for step in range(1, n_gy))
-    pf[...] = total[:, 0:3, :]
+    for c in range(3):
+        for b in range(own_blocks):
+            pf[c, b : b + 1, :] = total[b, c : c + 1, :]
     for step in range(1, group):
         tab(step).wait_send()
     swap.wait_send()
@@ -386,6 +399,16 @@
             x_down(t).wait_send()
 
         z_copy(t).wait_send()
+
+
+def write_out(new, forces, new_out, forces_out, sem):
+    copies = [pltpu.make_async_copy(forces, forces_out, sem.at[0])]
+    for c in range(new.shape[0]):
+        copies.append(pltpu.make_async_copy(new.at[c], new_out.at[c], sem.at[c + 1]))
+    for copy in copies:
+        copy.start()
+    for copy in copies:
+        copy.wait()
 
 
 def local(sizes, velocity, blade_pos, block_turbine, blade_vel, lift_coeff):
@@ -399,17 +422,17 @@
     rows = comps * depth * nrow
     dma = pltpu.SemaphoreType.DMA
     vmem = pl.BlockSpec(memory_space=pltpu.VMEM)
-    return pl.pallas_call(
+    by_comp = (blade_pos.shape[1], own_blocks, pts)
+    made = pl.pallas_call(
         functools.partial(kernel, sizes),
-        out_shape=(
-            jax.ShapeDtypeStruct(velocity.shape, F32),
-            jax.ShapeDtypeStruct(blade_pos.shape, F32),
-        ),
-        in_specs=[
-            pl.BlockSpec(memory_space=pl.ANY), vmem, pl.BlockSpec(memory_space=pltpu.SMEM), vmem, vmem,
-        ],
+        out_shape=(pltpu.VMEM(velocity.shape, F32), pltpu.VMEM(by_comp, F32)),
+        in_specs=[pl.BlockSpec(memory_space=pl.ANY)] * 5,
         out_specs=(vmem, vmem),
         scratch_shapes=[
+            pltpu.VMEM(by_comp, F32),
+            pltpu.SMEM((own_blocks,), jnp.int32),
+            pltpu.VMEM(by_comp, F32),
+            pltpu.VMEM((own_blocks, pts), F32),
             pltpu.VMEM((tiles + 2, comps, depth + 4, nrow + 16, LANES), F32),
             pltpu.VMEM((blocks, 8, pts), F32),
             pltpu.VMEM((ncol, count), BF16),
@@ -422,6 +445,7 @@
             pltpu.VMEM((8, count), F32),
             pltpu.VMEM((blocks, 8, pts), F32),
             pltpu.VMEM((n_gy, own_blocks, 8, pts), F32),
+            dma((4,)),
             dma((tiles,)),
             dma((group,)), dma((group,)),
             dma((tiles,)), dma((tiles,)),
@@ -431,10 +455,27 @@
             dma((n_gy,)), dma((n_gy,)),
         ],
         compiler_params=pltpu.CompilerParams(
-            collective_id=0, has_side_effects=True, vmem_limit_bytes=60 * 2**20
+            collective_id=0, has_side_effects=True, vmem_limit_bytes=44 * 2**20
         ),
         name="evolve",
-    )(velocity, blade_pos, block_turbine, blade_vel, lift_coeff)
+    )(
+        *(
+            pltpu.with_memory_space_constraint(arg, pltpu.HBM)
+            for arg in (
+                velocity, blade_pos.transpose(1, 0, 2), block_turbine, blade_vel.transpose(1, 0, 2), lift_coeff,
+            )
+        )
+    )
+    new, forces = pl.pallas_call(
+        write_out,
+        out_shape=(jax.ShapeDtypeStruct(velocity.shape, F32), jax.ShapeDtypeStruct(by_comp, F32)),
+        in_specs=[vmem, vmem],
+        out_specs=(pl.BlockSpec(memory_space=pl.ANY), pl.BlockSpec(memory_space=pl.ANY)),
+        scratch_shapes=[dma((comps + 1,))],
+        compiler_params=pltpu.CompilerParams(vmem_limit_bytes=16 * 2**20),
+        name="write_out",
+    )(*made)
+    return new, forces.transpose(1, 0, 2)
 
 
 def solution(mesh):

time: 55.9 us -> 46.1 us (0.82)
  local copies, waits for them, and re-layouts: 10.1 us -> 0 us
    unnamed x3 -> x0, local copies, waits for them, and re-layouts: 8.83 us -> none
    pallas_call x1 -> x0, local copies, waits for them, and re-layouts: 1.26 us -> none  [local(): pl.pallas_call(functools.partial(kernel, sizes), out_shape=(jax.ShapeDtyp...]
    pallas_call x1 -> x2, Pallas kernels: 44.9 us -> 45.3 us  [the longest x1 42.6 us: local(): pl.pallas_call(functools.partial(kernel, sizes), out_shape=(pltpu.VMEM(ve...]
where the time goes in v2:
time: 46.1 us; the launch traced here: 46 us
  Pallas kernels  45.3 us (98%)
  between operations  0.64 us (1%)
    pallas_call x1, Pallas kernels, local(): pl.pallas_call(functools.partial(kernel, sizes), out_shape=(pltpu.VMEM(ve...  42.6 us
    pallas_call x1, Pallas kernels, local(): pl.pallas_call(write_out, out_shape=(jax.ShapeDtypeStruct(velocity.shape,...  2.74 us

profile of v2, /device:TPU:25, one launch (start us, length us, event | category | flops | bytes accessed | tf_op | source)
XLA Modules:
  0.0 46.0 jit_solution(12219733251970548492)
XLA Ops:
  0.6 42.6 %evolve.1 = (f32[3,16,16,2048]{3,2,1,0:T(8,128)S(1)}, f32[3,2,128]{2,1,0:T(2,128)S(1)}) custom-call(f32[3,16,16,2048]{3,2,1,0:T(8,128)} %v.1, f32[3,2,128]{2,1,0:T(2,128)} %bitcast.3, s32[2]{0:T(128)} %turb_in.1, f32[3,2,128]{2,1,0:T(2,128)} %bitcast.4, f32[2,128]{1,0:T(2,128)} %lift_in.1), custom_call_target="tpu_custom_call" | custom-call | tf_op jit(solution)/shard_map/evolve/pallas_call | solution.py:426
  43.2 2.7 %write_out.1 = (f32[3,16,16,2048]{3,2,1,0:T(8,128)}, f32[3,2,128]{2,1,0:T(2,128)}) custom-call(f32[3,16,16,2048]{3,2,1,0:T(8,128)S(1)} %get-tuple-element.6.new, f32[3,2,128]{2,1,0:T(2,128)S(1)} %get-tuple-element.7.forces), custom_call_target="tpu_custom_call" | custom-call | tf_op jit(solution)/shard_map/write_out/pallas_call | solution.py:469

commit v3 on v2

--- a/solution.py
+++ b/solution.py
@@ -32,46 +32,48 @@
     return jnp.exp(gap * gap * (-1.0 / (smear * smear)))
 
 
-def stencil(win, tile, z, body):
+def spanwise(win, yd, yl, tile):
+    depth = win.shape[2] - 4
     lane = lax.broadcasted_iota(jnp.int32, (16, LANES), 1)
+    for z in range(depth):
+        for c in range(3):
+            left, u, right = (win[tile + side, c, z + 2, TOP : TOP + 16, :] for side in range(3))
+            p1 = pltpu.roll(jnp.where(lane < 1, right, u), LANES - 1, 1)
+            p2 = pltpu.roll(jnp.where(lane < 2, right, u), LANES - 2, 1)
+            m1 = pltpu.roll(jnp.where(lane >= LANES - 1, left, u), 1, 1)
+            m2 = pltpu.roll(jnp.where(lane >= LANES - 2, left, u), 2, 1)
+            yd[tile, z, c] = 8.0 * (p1 - m1) - (p2 - m2)
+            yl[tile, z, c] = 16.0 * (p1 + m1) - (p2 + m2) - 90.0 * u
+
+
+def stencil(win, yd, yl, tile, z, body):
     grads, laps, own = [], [], []
     for c in range(3):
-        def rows(offset, level=0, side=0, c=c):
-            return win[tile + side, c, z + level, TOP + offset : TOP + offset + 16, :]
+        def rows(offset, level=0, c=c):
+            return win[tile + 1, c, z + 2 + level, TOP + offset : TOP + offset + 16, :]
 
         u = rows(0)
-        left, right = rows(0, side=-1), rows(0, side=1)
-        y_p1 = pltpu.roll(jnp.where(lane < 1, right, u), LANES - 1, 1)
-        y_p2 = pltpu.roll(jnp.where(lane < 2, right, u), LANES - 2, 1)
-        y_m1 = pltpu.roll(jnp.where(lane >= LANES - 1, left, u), 1, 1)
-        y_m2 = pltpu.roll(jnp.where(lane >= LANES - 2, left, u), 2, 1)
-        pairs = (
-            (rows(1), rows(-1), rows(2), rows(-2)),
-            (y_p1, y_m1, y_p2, y_m2),
-            (rows(0, 1), rows(0, -1), rows(0, 2), rows(0, -2)),
-        )
-        grads.append([8.0 * (p1 - m1) - (p2 - m2) for p1, m1, p2, m2 in pairs])
-        near = sum(p1 + m1 for p1, m1, _, _ in pairs[1:]) + (pairs[0][0] + pairs[0][1])
-        far = sum(p2 + m2 for _, _, p2, m2 in pairs[1:]) + (pairs[0][2] + pairs[0][3])
-        laps.append(16.0 * near - far - 90.0 * u)
+        x_p1, x_m1, x_p2, x_m2 = rows(1), rows(-1), rows(2), rows(-2)
+        z_p1, z_m1, z_p2, z_m2 = rows(0, 1), rows(0, -1), rows(0, 2), rows(0, -2)
+        grads.append([8.0 * (x_p1 - x_m1) - (x_p2 - x_m2), yd[tile, z, c], 8.0 * (z_p1 - z_m1) - (z_p2 - z_m2)])
+        near = (x_p1 + x_m1) + (z_p1 + z_m1)
+        far = (x_p2 + x_m2) + (z_p2 + z_m2)
+        laps.append((16.0 * near - far) + yl[tile, z, c])
         own.append(u)
-    diag = sum(grads[i][i] * grads[i][i] for i in range(3))
-    cross = jnp.zeros((16, LANES), F32)
-    for i, j in ((0, 1), (0, 2), (1, 2)):
-        both = grads[i][j] + grads[j][i]
-        cross = cross + both * both
-    strain = diag + diag + cross
+    diag = grads[0][0] * grads[0][0] + grads[1][1] * grads[1][1] + grads[2][2] * grads[2][2]
+    both = [grads[i][j] + grads[j][i] for i, j in ((0, 1), (0, 2), (1, 2))]
+    cross = both[0] * both[0] + both[1] * both[1] + both[2] * both[2]
+    strain = (diag + diag) + cross
     nu = viscosity * time_step / 12.0 + (smag_coeff * smag_coeff * time_step / 144.0) * jnp.sqrt(strain)
-    outs = []
-    for c in range(3):
-        outs.append(own[c] + (-mean_wind * time_step / 12.0) * grads[c][0] + nu * laps[c] + time_step * body[c])
-    return outs
+    return [
+        own[c] + (-mean_wind * time_step / 12.0) * grads[c][0] + nu * laps[c] + time_step * body[c] for c in range(3)
+    ]
 
 
 def kernel(
     sizes, v, pos_in, turb_in, bvel_in, lift_in, out, pf,
     pos, turb, bvel, lift,
-    win, table, whi, wlo, along, plane, ghi, glo, part, other, back, owned,
+    win, vhi, vlo, yd, yl, table, whi, wlo, along, plane, ghi, glo, part, other, back, owned,
     small_sem, load_sem, tab_send, tab_recv, z_send, z_recv, x_send, x_recv, y_send, y_recv,
     part_sem, back_send, back_recv,
 ):
@@ -231,6 +233,13 @@
 
         z_copy(t).start()
 
+    @pl.loop(0, tiles)
+    def _(t):
+        load(t).wait()
+        high, low = split(win[t + 1, :, 2 : 2 + depth, TOP : TOP + nrow, :].reshape(rows, LANES))
+        vhi[t] = high
+        vlo[t] = low
+
     for step in range(1, group):
         tab(step).wait_recv()
     turbine = gy.astype(F32)
@@ -256,34 +265,23 @@
         plane[z * nrow : (z + 1) * nrow, :] = weight_z[z : z + 1, :] * weight_x
     center_y = flat(1)
 
-    step_cols = 2 * LANES
+    per_step = 4
+    step_cols = per_step * LANES
     steps = ncol // step_cols
 
-    @pl.loop(0, steps)
-    def _(j):
-        at = pl.multiple_of(j * step_cols, step_cols)
+    for j in range(steps):
+        at = j * step_cols
         high, low = split(gaussian(gy * ncol + at, step_cols, center_y))
-        whi[pl.ds(at, step_cols), :] = high
-        wlo[pl.ds(at, step_cols), :] = low
-        load(2 * j).wait()
-        load(2 * j + 1).wait()
-        cells = jnp.concatenate(
-            [
-                win[2 * j + 1 + k, :, 2 : 2 + depth, TOP : TOP + nrow, :].reshape(rows, LANES)
-                for k in range(2)
-            ],
-            axis=1,
-        )
-        vhi, vlo = split(cells)
+        whi[at : at + step_cols, :] = high
+        wlo[at : at + step_cols, :] = low
+        vh, vl = (
+            jnp.concatenate([term[per_step * j + k] for k in range(per_step)], axis=1) for term in (vhi, vlo)
+        )
         dot = functools.partial(jnp.dot, preferred_element_type=F32)
-        now = dot(vhi, high) + (dot(vhi, low) + dot(vlo, high))
-
-        @pl.when(j == 0)
-        def _():
+        now = dot(jnp.concatenate([vh, vl], axis=1), jnp.concatenate([high, high], axis=0)) + dot(vh, low)
+        if j == 0:
             along[...] = now
-
-        @pl.when(j > 0)
-        def _():
+        else:
             along[...] += now
 
     per_comp = depth * nrow
@@ -341,9 +339,14 @@
         def dot(a, b):
             return lax.dot_general(a, b, (((1,), (1,)), ((), ())), preferred_element_type=F32)
 
-        along[:, 0:step_cols] = dot(ghi[...], high) + (dot(ghi[...], low) + dot(glo[...], high))
-        for k in range(2):
-            t = 2 * j + k
+        both = jnp.concatenate([ghi[...], glo[...]], axis=1)
+        along[...] = dot(both, jnp.concatenate([high, high], axis=1)) + dot(ghi[...], low)
+        for k in range(per_step):
+            spanwise(win, yd, yl, per_step * j + k)
+
+        @pl.loop(0, per_step)
+        def _(k):
+            t = per_step * j + k
 
             @pl.when(gx > 0)
             def _():
@@ -354,21 +357,14 @@
                 x_down(t).wait_recv()
 
             z_copy(t).wait_recv()
-
-            @pl.loop(0, depth // 4)
-            def _(zb):
-                for dz in range(4):
-                    z = zb * 4 + dz
-                    body = [
-                        along[
-                            pl.ds(pl.multiple_of(c * per_comp + z * nrow, nrow), nrow),
-                            k * LANES : (k + 1) * LANES,
-                        ]
-                        for c in range(3)
-                    ]
-                    new = stencil(win, t + 1, z + 2, body)
-                    for c in range(3):
-                        out[c, z, :, lanes(t)] = new[c]
+            for z in range(depth):
+                body = [
+                    along[c * per_comp + z * nrow : c * per_comp + (z + 1) * nrow, lanes(k)]
+                    for c in range(3)
+                ]
+                new = stencil(win, yd, yl, t, z, body)
+                for c in range(3):
+                    out[c, z, :, lanes(t)] = new[c]
 
     for step in range(1, n_gy):
         give(step).wait()
@@ -434,6 +430,10 @@
             pltpu.VMEM(by_comp, F32),
             pltpu.VMEM((own_blocks, pts), F32),
             pltpu.VMEM((tiles + 2, comps, depth + 4, nrow + 16, LANES), F32),
+            pltpu.VMEM((tiles, rows, LANES), BF16),
+            pltpu.VMEM((tiles, rows, LANES), BF16),
+            pltpu.VMEM((tiles, depth, comps, nrow, LANES), F32),
+            pltpu.VMEM((tiles, depth, comps, nrow, LANES), F32),
             pltpu.VMEM((blocks, 8, pts), F32),
             pltpu.VMEM((ncol, count), BF16),
             pltpu.VMEM((ncol, count), BF16),
@@ -455,7 +455,7 @@
             dma((n_gy,)), dma((n_gy,)),
         ],
         compiler_params=pltpu.CompilerParams(
-            collective_id=0, has_side_effects=True, vmem_limit_bytes=44 * 2**20
+            collective_id=0, has_side_effects=True, vmem_limit_bytes=54 * 2**20
         ),
         name="evolve",
     )(

time: 46.1 us -> 34.7 us (0.75)
  Pallas kernels: 45.3 us -> 33.9 us
    pallas_call x1, Pallas kernels: 42.6 us -> 31.2 us  [local(): pl.pallas_call(functools.partial(kernel, sizes), out_shape=(pltpu.VMEM(ve...]
where the time goes in v3:
time: 34.7 us; the launch traced here: 34.6 us
  Pallas kernels  33.9 us (98%)
  between operations  0.64 us (2%)
    pallas_call x1, Pallas kernels, local(): pl.pallas_call(functools.partial(kernel, sizes), out_shape=(pltpu.VMEM(ve...  31.2 us
    pallas_call x1, Pallas kernels, local(): pl.pallas_call(write_out, out_shape=(jax.ShapeDtypeStruct(velocity.shape,...  2.74 us

profile of v3, /device:TPU:25, one launch (start us, length us, event | category | flops | bytes accessed | tf_op | source)
XLA Modules:
  0.0 34.6 jit_solution(5717827503555538880)
XLA Ops:
  0.6 31.2 %evolve.1 = (f32[3,16,16,2048]{3,2,1,0:T(8,128)S(1)}, f32[3,2,128]{2,1,0:T(2,128)S(1)}) custom-call(f32[3,16,16,2048]{3,2,1,0:T(8,128)} %v.1, f32[3,2,128]{2,1,0:T(2,128)} %bitcast.3, s32[2]{0:T(128)} %turb_in.1, f32[3,2,128]{2,1,0:T(2,128)} %bitcast.4, f32[2,128]{1,0:T(2,128)} %lift_in.1), custom_call_target="tpu_custom_call" | custom-call | tf_op jit(solution)/shard_map/evolve/pallas_call | solution.py:422
  31.8 2.7 %write_out.1 = (f32[3,16,16,2048]{3,2,1,0:T(8,128)}, f32[3,2,128]{2,1,0:T(2,128)}) custom-call(f32[3,16,16,2048]{3,2,1,0:T(8,128)S(1)} %get-tuple-element.6.new, f32[3,2,128]{2,1,0:T(2,128)S(1)} %get-tuple-element.7.forces), custom_call_target="tpu_custom_call" | custom-call | tf_op jit(solution)/shard_map/write_out/pallas_call | solution.py:469

commit v4 on v3

--- a/solution.py
+++ b/solution.py
@@ -18,6 +18,7 @@
 F32, BF16 = jnp.float32, jnp.bfloat16
 MESH = pl.DeviceIdType.MESH
 LANES = 128
+TINY = float(jnp.finfo(F32).tiny)
 TOP = 8
 
 
@@ -64,9 +65,11 @@
     both = [grads[i][j] + grads[j][i] for i, j in ((0, 1), (0, 2), (1, 2))]
     cross = both[0] * both[0] + both[1] * both[1] + both[2] * both[2]
     strain = (diag + diag) + cross
-    nu = viscosity * time_step / 12.0 + (smag_coeff * smag_coeff * time_step / 144.0) * jnp.sqrt(strain)
+    nu = viscosity * time_step / 12.0 + (smag_coeff * smag_coeff * time_step / 144.0) * (
+        strain * lax.rsqrt(jnp.maximum(strain, TINY))
+    )
     return [
-        own[c] + (-mean_wind * time_step / 12.0) * grads[c][0] + nu * laps[c] + time_step * body[c] for c in range(3)
+        own[c] + (-mean_wind * time_step / 12.0) * grads[c][0] + nu * laps[c] + body[c] for c in range(3)
     ]
 
 
@@ -319,7 +322,7 @@
         give(step).start()
 
     for c in range(3):
-        high, low = split((smear_norm * force[c]) * plane[...])
+        high, low = split((time_step * smear_norm * force[c]) * plane[...])
         ghi[c * per_comp : (c + 1) * per_comp, :] = high
         glo[c * per_comp : (c + 1) * per_comp, :] = low
 

time: 34.7 us -> 34.6 us (level)
  no operation moved by 1% of the time
where the time goes in v4:
time: 34.6 us; the launch traced here: 34.5 us
  Pallas kernels  33.8 us (98%)
  between operations  0.64 us (2%)
    pallas_call x1, Pallas kernels, local(): pl.pallas_call(functools.partial(kernel, sizes), out_shape=(pltpu.VMEM(ve...  31.1 us
    pallas_call x1, Pallas kernels, local(): pl.pallas_call(write_out, out_shape=(jax.ShapeDtypeStruct(velocity.shape,...  2.74 us

profile of v4, /device:TPU:25, one launch (start us, length us, event | category | flops | bytes accessed | tf_op | source)
XLA Modules:
  0.0 34.5 jit_solution(9840267435418057378)
XLA Ops:
  0.6 31.1 %evolve.1 = (f32[3,16,16,2048]{3,2,1,0:T(8,128)S(1)}, f32[3,2,128]{2,1,0:T(2,128)S(1)}) custom-call(f32[3,16,16,2048]{3,2,1,0:T(8,128)} %v.1, f32[3,2,128]{2,1,0:T(2,128)} %bitcast.3, s32[2]{0:T(128)} %turb_in.1, f32[3,2,128]{2,1,0:T(2,128)} %bitcast.4, f32[2,128]{1,0:T(2,128)} %lift_in.1), custom_call_target="tpu_custom_call" | custom-call | tf_op jit(solution)/shard_map/evolve/pallas_call | solution.py:425
  31.7 2.7 %write_out.1 = (f32[3,16,16,2048]{3,2,1,0:T(8,128)}, f32[3,2,128]{2,1,0:T(2,128)}) custom-call(f32[3,16,16,2048]{3,2,1,0:T(8,128)S(1)} %get-tuple-element.6.new, f32[3,2,128]{2,1,0:T(2,128)S(1)} %get-tuple-element.7.forces), custom_call_target="tpu_custom_call" | custom-call | tf_op jit(solution)/shard_map/write_out/pallas_call | solution.py:472

commit v5 on v4

--- a/solution.py
+++ b/solution.py
@@ -30,7 +30,7 @@
 def gaussian(start, count, centers):
     cells = (lax.broadcasted_iota(jnp.int32, (count, 1), 0) + start).astype(F32)
     gap = cells - centers
-    return jnp.exp(gap * gap * (-1.0 / (smear * smear)))
+    return jnp.exp2(gap * gap * (-math.log2(math.e) / (smear * smear)))
 
 
 def spanwise(win, yd, yl, tile):

time: 34.6 us -> 34.6 us (level)
  no operation moved by 1% of the time
where the time goes in v5:
time: 34.6 us; the launch traced here: 34.5 us
  Pallas kernels  33.8 us (98%)
  between operations  0.64 us (2%)
    pallas_call x1, Pallas kernels, local(): pl.pallas_call(functools.partial(kernel, sizes), out_shape=(pltpu.VMEM(ve...  31.1 us
    pallas_call x1, Pallas kernels, local(): pl.pallas_call(write_out, out_shape=(jax.ShapeDtypeStruct(velocity.shape,...  2.74 us

profile of v5, /device:TPU:25, one launch (start us, length us, event | category | flops | bytes accessed | tf_op | source)
XLA Modules:
  0.0 34.5 jit_solution(8940719829850566545)
XLA Ops:
  0.6 31.1 %evolve.1 = (f32[3,16,16,2048]{3,2,1,0:T(8,128)S(1)}, f32[3,2,128]{2,1,0:T(2,128)S(1)}) custom-call(f32[3,16,16,2048]{3,2,1,0:T(8,128)} %v.1, f32[3,2,128]{2,1,0:T(2,128)} %bitcast.3, s32[2]{0:T(128)} %turb_in.1, f32[3,2,128]{2,1,0:T(2,128)} %bitcast.4, f32[2,128]{1,0:T(2,128)} %lift_in.1), custom_call_target="tpu_custom_call" | custom-call | tf_op jit(solution)/shard_map/evolve/pallas_call | solution.py:425
  31.7 2.7 %write_out.1 = (f32[3,16,16,2048]{3,2,1,0:T(8,128)}, f32[3,2,128]{2,1,0:T(2,128)}) custom-call(f32[3,16,16,2048]{3,2,1,0:T(8,128)S(1)} %get-tuple-element.6.new, f32[3,2,128]{2,1,0:T(2,128)S(1)} %get-tuple-element.7.forces), custom_call_target="tpu_custom_call" | custom-call | tf_op jit(solution)/shard_map/write_out/pallas_call | solution.py:472
